TPU v7x, 256 devices: a whole 4x4x8 slice. The times are simulated.
256 devices in a mesh: replica: 16 (over y, z_lo, core), fsdp: 16 (over x, z_hi).
Axes of the slice: x: 4, y: 4, z: 8 (z_hi: 4, z_lo: 2; z = z_hi * 2 + z_lo), core: 2. Of those that a mesh axis runs over, the one named last changes fastest.
Arguments:
- activations: bfloat16 [16, 10240, 4608], P('replica', 'fsdp'), may hold values from -6 to 6
- teacher: bfloat16 [16, 10240, 1024], P('replica', 'fsdp'), may hold values from -6 to 6
- weights: float32 [16, 4608, 1024], P('replica', 'fsdp'), may hold values from -6 to 6
- first_moment: float32 [16, 4608, 1024], P('replica', 'fsdp'), may hold values from -0.001953125 to 0.001953125
- second_moment: float32 [16, 4608, 1024], P('replica', 'fsdp'), may hold values from 2.1192763e-10 to 2.1192763e-08
- anchor: float32 [4, 4608, 256], P(None, 'fsdp', 'replica'), may hold values from -6 to 6
- momentum: float32 [4, 4608, 256], P(None, 'fsdp', 'replica'), may hold values from -6 to 6
- fragment: int32 [1], replicated, may hold values from 0 to 255
Outputs:
- new_weights: float32 [16, 4608, 1024], P('replica', 'fsdp')
- new_anchor: float32 [4, 4608, 256], P(None, 'fsdp', 'replica')
- new_momentum: float32 [4, 4608, 256], P(None, 'fsdp', 'replica')
All inputs are finite; a program needn't handle non-finite values.
Results may differ from a plain program's by a relative error of at most 0.007.
Values may be sent and summed in bfloat16 or wider, within the bound.
A program may use at most 128 MiB of HBM per device.

v0:
```python
import math

import jax
import jax.numpy as jnp
from jax import lax
from jax.sharding import PartitionSpec as P

FRAGS = 4
WINDOWS = 256


def shards(activations, teacher, weights, first_moment, second_moment, anchor, momentum, fragment):
    inputs = activations[0]
    target = teacher[0]
    master = weights[0]
    scale = 1.0 / math.sqrt(inputs.shape[1])
    window = fragment[0]
    index = jnp.remainder(window, FRAGS)
    outer_rate = 0.4 + 0.6 * window.astype(jnp.float32) / WINDOWS
    replicas = lax.axis_size("replica")
    share = anchor.shape[2]
    width = share * replicas
    start_col = index * width
    old_block = lax.dynamic_slice_in_dim(master, start_col, width, 1)
    own_anchor = lax.dynamic_index_in_dim(anchor, index, 0, keepdims=False)
    own_moment = lax.dynamic_index_in_dim(momentum, index, 0, keepdims=False)
    anchor_full, moment_full = (
        lax.all_gather(own_anchor.astype(jnp.bfloat16), "replica", axis=1, tiled=True).astype(
            own_anchor.dtype
        ),
        lax.all_gather(own_moment.astype(jnp.bfloat16), "replica", axis=1, tiled=True).astype(
            own_moment.dtype
        ),
    )
    total = lax.psum(old_block.astype(jnp.bfloat16), "replica").astype(jnp.float32)
    outer_whole = anchor_full - total / replicas
    moment_whole = 0.9 * moment_full + outer_whole
    anchor_whole = anchor_full - outer_rate * (outer_whole + 0.9 * moment_whole)
    offset = lax.axis_index("replica") * share
    moment_next = lax.dynamic_slice_in_dim(moment_whole, offset, share, 1)
    anchor_next = lax.dynamic_slice_in_dim(anchor_whole, offset, share, 1)
    low = master.astype(jnp.bfloat16)
    columns = inputs
    values = (
        jnp.dot(
            columns,
            lax.all_gather(low, "fsdp", axis=0, tiled=True),
            preferred_element_type=jnp.float32,
        )
        * scale
    )
    batch = inputs.shape[0] * lax.axis_size("fsdp")
    error = ((values - target.astype(jnp.float32)) / batch).astype(jnp.bfloat16)
    columns = inputs
    grad = (
        lax.psum_scatter(
            lax.dot_general(
                columns, error, (((0,), (0,)), ((), ())), preferred_element_type=jnp.float32
            ).astype(jnp.bfloat16),
            "fsdp",
            scatter_dimension=0,
            tiled=True,
        ).astype(jnp.float32)
        * scale
    )
    moment1 = 0.9 * first_moment[0] + 0.1 * grad
    moment2 = 0.95 * second_moment[0] + 0.05 * grad * grad
    stepped = master - 0.25 * (moment1 / (jnp.sqrt(moment2) + 1e-08) + 0.1 * master)
    mixed = 0.5 * anchor_whole + 0.5 * lax.dynamic_slice_in_dim(stepped, start_col, width, 1)
    new_weights = lax.dynamic_update_slice_in_dim(stepped, mixed, start_col, 1)
    new_anchor = lax.dynamic_update_index_in_dim(anchor, anchor_next, index, 0)
    new_momentum = lax.dynamic_update_index_in_dim(momentum, moment_next, index, 0)
    return (new_weights[None], new_anchor, new_momentum)


def solution(mesh):
    in_specs = (
        P("replica", "fsdp", None),
        P("replica", "fsdp", None),
        P("replica", "fsdp", None),
        P("replica", "fsdp", None),
        P("replica", "fsdp", None),
        P(None, "fsdp", "replica"),
        P(None, "fsdp", "replica"),
        P(),
    )
    out_specs = (P("replica", "fsdp", None), P(None, "fsdp", "replica"), P(None, "fsdp", "replica"))
    return jax.shard_map(shards, mesh=mesh, in_specs=in_specs, out_specs=out_specs, check_vma=False)
```

profile of v0, /device:TPU:32, one launch (start us, length us, event | category | flops | bytes accessed | tf_op | source)
XLA Modules:
  0.0 327.2 jit_solution(11738576606107982344)
XLA Ops:
  8.0 0.0 all-gather.4.cloned.1.call-start
  8.0 0.9 copy.35
  8.9 0.0 copy-start.1
  8.9 0.9 copy.34
  9.9 0.0 copy-start.2
  9.9 1.8 copy.19
  11.6 0.1 bitcast_convert_fusion
  11.7 1.1 copy.21
  12.8 0.0 all-gather.4.cloned.1.call-update
  12.8 0.0 all-reduce.2.cloned.1.call-start
  13.6 0.7 fusion.17
  14.3 0.0 all-reduce.2.cloned.1.call-update
  14.3 0.0 reduce-scatter.4.cloned.1.call-start
  14.4 128.1 %all-gather.4.cloned.1.call-done = bf16[4608,1024]{1,0:T(8,128)(2,1)} async-done(((bf16[288,1024]{1,0:T(8,128)(2,1)}), bf16[4608,1024]{1,0:T(8,128)(2,1)}) %all-gather.4.cloned.1.call-update) | async-done | bytes 9437200 | tf_op jit(solution)/shard_map/all_gather | solution.py:47
  142.4 10.8 %fusion.5 = bf16[640,1024]{1,0:T(8,128)(2,1)S(1)} fusion(bf16[4608,1024]{1,0:T(8,128)(2,1)} %all-gather.4.cloned.1.call-done, bf16[1,640,4608]{2,1,0:T(8,128)(2,1)} %param.8, bf16[1,640,1024]{2,1,0:T(8,128)(2,1)} %param.9), kind=kOutput, calls=%fused_computation.7 | convolution fusion | flops 6043074560 | bytes 17956864 | tf_op jit(solution)/shard_map/dot_general | solution.py:45
  153.3 12.6 %fusion = bf16[4608,1024]{0,1:T(8,128)(2,1)} fusion(bf16[640,1024]{1,0:T(8,128)(2,1)S(1)} %fusion.5, bf16[1,640,4608]{2,1,0:T(8,128)(2,1)} %param.8), kind=kOutput, calls=%fused_computation.1 | convolution fusion | flops 6044516352 | bytes 16646144 | tf_op jit(solution)/shard_map/dot_general | solution.py:57
  165.9 12.7 %copy.25 = bf16[4608,1024]{1,0:T(8,128)(2,1)} copy(bf16[4608,1024]{0,1:T(8,128)(2,1)} %fusion) | data formatting | bytes 18874368
  178.6 0.0 reduce-scatter.4.cloned.1.call-update
  178.7 1.7 copy.22
  180.4 2.9 copy.20
  183.3 0.0 copy-done.1
  183.3 20.9 %all-gather.1 = bf16[1,288,256]{1,2,0:T(8,128)(2,1)S(1)} all-gather(bf16[1,288,16]{1,2,0:T(8,128)(2,1)S(1)} %dynamic-slice_convert_fusion.1), channel_id=3, replica_groups=mesh['replica'=16,'fsdp'=16] {'replica'}, dimensions={2}, use_global_device_ids=true | all-gather | bytes 156672 | tf_op jit(solution)/shard_map/all_gather | solution.py:31
  204.2 0.0 copy-done.2
  204.2 23.5 %all-gather = bf16[1,288,256]{1,2,0:T(8,128)(2,1)S(1)} all-gather(bf16[1,288,16]{1,2,0:T(8,128)(2,1)S(1)} %dynamic-slice_convert_fusion.2), channel_id=2, replica_groups=mesh['replica'=16,'fsdp'=16] {'replica'}, dimensions={2}, use_global_device_ids=true | all-gather | bytes 156672 | tf_op jit(solution)/shard_map/all_gather | solution.py:28
  227.8 0.0 all-reduce.2.cloned.1.call-done
  227.8 1.8 bitcast_add_fusion
  229.6 81.2 %reduce-scatter.4.cloned.1.call-done = bf16[288,1024]{1,0:T(8,128)(2,1)} async-done(((bf16[4608,1024]{1,0:T(8,128)(2,1)}), bf16[288,1024]{1,0:T(8,128)(2,1)}) %reduce-scatter.4.cloned.1.call-update) | async-done | bytes 589840
  310.8 2.2 copy.26
  313.0 2.8 fusion.12
  315.8 0.0 copy-start
  315.8 0.1 copy.28
  316.0 0.8 copy-done
  316.8 0.2 bitcast_dynamic-update-slice_fusion
  316.9 1.5 copy.24
  318.4 1.4 bitcast_dynamic-update-slice_fusion.1
  (2 shorter events, 0.0 us)
Async XLA Ops:
  8.0 134.4 %all-gather.4.cloned.1.call-start = ((), (), s32[]{:S(2)}) async-start(), calls=%async_computation.1 | async-start | bytes 10027008 | tf_op jit(solution)/shard_map/all_gather | solution.py:47
  8.9 174.4 %copy-start.1 = (f32[4,288,16]{1,2,0:T(8,128)}, f32[4,288,16]{1,2,0:T(8,128)S(1)}, u32[]{:S(2)}) copy-start(f32[4,288,16]{1,2,0:T(8,128)S(1)} %copy.35) | copy-start | bytes 221188
  9.9 194.4 %copy-start.2 = (f32[4,288,16]{1,2,0:T(8,128)}, f32[4,288,16]{1,2,0:T(8,128)S(1)}, u32[]{:S(2)}) copy-start(f32[4,288,16]{1,2,0:T(8,128)S(1)} %copy.34) | copy-start | bytes 221188
  12.8 214.9 %all-reduce.2.cloned.1.call-start = ((), (), s32[]{:S(2)}) async-start(), calls=%async_computation.2 | async-start | bytes 393216 | tf_op jit(solution)/shard_map/psum | solution.py:35
  14.3 296.5 %reduce-scatter.4.cloned.1.call-start = ((), (), s32[]{:S(2)}) async-start(), calls=%async_computation.3 | async-start | bytes 10027008
  315.8 0.9 copy-start
Sparse Core Ops, SparseCore 0:
  13.0 129.4 all-gather.3
  178.8 131.9 reduce-scatter.3
Sparse Core Ops, SparseCore 1:
  16.1 210.1 all-reduce.1
where the time goes:
time: 329 us; the launch traced here: 327 us
  waiting for transfers between devices  209 us (64%)
  blocking collectives  44.5 us (14%)
  local copies, waits for them, and re-layouts  28.7 us (9%)
  matrix products  23.5 us (7%)
  between operations  16.2 us (5%)
  other arithmetic  4.87 us (1%)
    all_gather x1, waiting for transfers between devices, shards(): lax.all_gather(low, 'fsdp', axis=0, tiled=True)  128 us
    unnamed x4, waiting for transfers between devices  81.3 us
    unnamed x15, local copies, waits for them, and re-layouts  25.6 us
    all_gather x1, blocking collectives, shards(): lax.all_gather(own_anchor.astype(jnp.bfloat16), 'replica', axis=1, tiled=...  23.5 us
    all_gather x1, blocking collectives, shards(): lax.all_gather(own_moment.astype(jnp.bfloat16), 'replica', axis=1, tiled=...  20.9 us
    dot_general x1, matrix products, shards(): lax.dot_general(columns, error, (((0,), (0,)), ((), ())), preferred_eleme...  12.6 us
    dot_general x1, matrix products, shards(): jnp.dot(columns, lax.all_gather(low, 'fsdp', axis=0, tiled=True), preferr...  10.8 us
  transfers between devices with their start and end apart: 3, of which 2 were waited for; matrix products, arithmetic and copies ran while one was open for 13% of the time, Pallas kernels for 0%

commit v1 on v0

v1 whole, which is shorter than its diff:
```python
import functools
import math

import jax
import jax.numpy as jnp
from jax import lax
from jax.experimental import pallas as pl
from jax.experimental.pallas import tpu as pltpu
from jax.sharding import PartitionSpec as P

FRAGS = 4
WINDOWS = 256
SIDE = 4
CHUNKS = 4
ROWS_A = 224
LANES = 384
MESH = pl.DeviceIdType.MESH
F32 = jnp.float32
BF16 = jnp.bfloat16


def kernel(
    batch,
    frag_ref,
    act_hbm,
    tgt_hbm,
    w_hbm,
    m1_hbm,
    m2_hbm,
    anc_ref,
    mom_ref,
    nw_hbm,
    na_ref,
    nm_ref,
    act,
    act_t,
    tgt,
    w,
    m1,
    m2,
    nw,
    wf,
    pt,
    err,
    acc,
    rxh,
    rxf,
    rzh,
    rzf,
    bzh,
    bzf,
    bxh,
    bxf,
    tall,
    old_t,
    anc_t,
    anc_full,
    got,
    in_sem,
    out_sem,
    ssem,
    rsem,
    osend,
    orecv,
):
    nc, rows, cw = wf.shape[0], wf.shape[3], wf.shape[4]
    ra, rb = ROWS_A, rows - ROWS_A
    ha, hb = ra // 2, rb // 2
    depth = act.shape[1]
    scale = 1.0 / math.sqrt(depth)
    group = SIDE * rows

    me = lax.axis_index("fsdp")
    rep = lax.axis_index("replica")
    replicas = lax.axis_size("replica")
    x, z = lax.div(me, SIDE), lax.rem(me, SIDE)
    xp, xm, x2 = (lax.rem(x + k, SIDE) for k in (1, 3, 2))
    zp, zm, z2 = (lax.rem(z + k, SIDE) for k in (1, 3, 2))
    x_to = [xp * SIDE + z, xm * SIDE + z]
    z_to = [x * SIDE + zp, x * SIDE + zm]
    bits = []
    step = replicas // 2
    while step:
        bits.append(step)
        step //= 2
    halves = [lax.rem(lax.div(rep, b), 2) for b in bits]
    partners = [rep + b - 2 * b * h for b, h in zip(bits, halves)]

    barrier = pltpu.get_barrier_semaphore()
    for to in x_to + z_to:
        pl.semaphore_signal(barrier, inc=1, device_id={"fsdp": to}, device_id_type=MESH)
    for to in partners:
        pl.semaphore_signal(barrier, inc=1, device_id={"replica": to}, device_id_type=MESH)

    loads = [
        pltpu.make_async_copy(src, dst, in_sem.at[k])
        for k, (src, dst) in enumerate(
            [(w_hbm, w), (act_hbm, act), (tgt_hbm, tgt), (m1_hbm, m1), (m2_hbm, m2)]
        )
    ]
    for load in loads:
        load.start()

    top, low_half, high_half = pl.ds(0, ra), pl.ds(0, ha), pl.ds(ha, ha)
    end, low_end, high_end = pl.ds(ra, rb), pl.ds(ra, hb), pl.ds(ra + hb, hb)
    every = pl.ds(0, SIDE)
    sent = {}

    def send(c, phase, pairs, to):
        copies = []
        for d in range(2):
            src, dst = pairs[d]
            copies.append(
                pltpu.make_async_remote_copy(
                    src_ref=src,
                    dst_ref=dst,
                    send_sem=ssem.at[c, phase, d],
                    recv_sem=rsem.at[c, phase, d],
                    device_id={"fsdp": to[d]},
                    device_id_type=MESH,
                )
            )
        for copy in copies:
            copy.start()
        sent[c, phase] = copies

    def arrive(c, phase):
        for copy in sent[c, phase]:
            copy.wait_recv()

    def same(*refs):
        return [(r, r) for r in refs]

    def cols(c):
        return pl.ds(c * cw, cw)

    def a0(c):
        wf[c, x, z] = w[:, cols(c)].astype(BF16)
        own = wf.at[c, x, z, top]
        send(c, 0, same(own, own), z_to)
        own = wf.at[c, x, z, end]
        send(c, 1, same(own, own), x_to)

    def a1(c):
        arrive(c, 0)
        send(c, 2, same(wf.at[c, x, zm, low_half], wf.at[c, x, zp, high_half]), z_to)
        arrive(c, 1)
        send(c, 3, same(wf.at[c, xm, z, low_end], wf.at[c, xp, z, high_end]), x_to)

    def a2(c):
        arrive(c, 2)
        own = wf.at[c, x, every, top]
        send(c, 4, same(own, own), x_to)
        arrive(c, 3)
        own = wf.at[c, every, z, end]
        send(c, 5, same(own, own), z_to)

    def a3(c):
        arrive(c, 4)
        send(c, 6, same(wf.at[c, xm, every, low_half], wf.at[c, xp, every, high_half]), x_to)
        arrive(c, 5)
        send(c, 7, same(wf.at[c, every, zm, low_end], wf.at[c, every, zp, high_end]), z_to)

    def a4(c):
        arrive(c, 6)
        arrive(c, 7)

    def compute(c):
        total = None
        for g in range(SIDE):
            term = jnp.dot(
                act[:, pl.ds(g * group, group)],
                wf[c, g].reshape(group, cw),
                preferred_element_type=F32,
            )
            total = term if total is None else total + term
        values = total * scale
        err[...] = ((values - tgt[:, cols(c)].astype(F32)) / batch).astype(BF16)
        for g in (x2, xp, xm, x):
            part = jnp.dot(
                act_t[pl.ds(pl.multiple_of(g * group, group), group), :],
                err[...],
                preferred_element_type=F32,
            )
            pt[c, g] = part.astype(BF16).reshape(SIDE, rows, cw)
            if g is x2:
                send(
                    c,
                    8,
                    [
                        (pt.at[c, x2, every, low_half], rxh.at[c, 0]),
                        (pt.at[c, x2, every, high_half], rxh.at[c, 1]),
                    ],
                    x_to,
                )
        send(
            c,
            9,
            [
                (pt.at[c, every, z2, low_end], bzh.at[c, 0]),
                (pt.at[c, every, z2, high_end], bzh.at[c, 1]),
            ],
            z_to,
        )

    def add(c, i, j, part, *terms):
        total = pt[c, i, j, part, :].astype(F32)
        for term in terms:
            total = total + term.astype(F32)
        pt[c, i, j, part, :] = total.astype(BF16)

    def r1(c):
        arrive(c, 8)
        for k in range(SIDE):
            add(c, xp, k, low_half, rxh[c, 0, k])
            add(c, xm, k, high_half, rxh[c, 1, k])
        send(
            c,
            10,
            [
                (pt.at[c, xp, every, top], rxf.at[c, 0]),
                (pt.at[c, xm, every, top], rxf.at[c, 1]),
            ],
            x_to,
        )
        arrive(c, 9)
        for k in range(SIDE):
            add(c, k, zp, low_end, bzh[c, 0, k])
            add(c, k, zm, high_end, bzh[c, 1, k])
        send(
            c,
            11,
            [
                (pt.at[c, every, zp, end], bzf.at[c, 0]),
                (pt.at[c, every, zm, end], bzf.at[c, 1]),
            ],
            z_to,
        )

    def r2(c):
        arrive(c, 10)
        for k in range(SIDE):
            add(c, x, k, top, rxf[c, 0, k], rxf[c, 1, k])
        send(
            c,
            12,
            [
                (pt.at[c, x, z2, low_half], rzh.at[c, 0]),
                (pt.at[c, x, z2, high_half], rzh.at[c, 1]),
            ],
            z_to,
        )
        arrive(c, 11)
        for k in range(SIDE):
            add(c, k, z, end, bzf[c, 0, k], bzf[c, 1, k])
        send(
            c,
            13,
            [
                (pt.at[c, x2, z, low_end], bxh.at[c, 0]),
                (pt.at[c, x2, z, high_end], bxh.at[c, 1]),
            ],
            x_to,
        )

    def r3(c):
        arrive(c, 12)
        add(c, x, zp, low_half, rzh[c, 0])
        add(c, x, zm, high_half, rzh[c, 1])
        send(
            c,
            14,
            [(pt.at[c, x, zp, top], rzf.at[c, 0]), (pt.at[c, x, zm, top], rzf.at[c, 1])],
            z_to,
        )
        arrive(c, 13)
        add(c, xp, z, low_end, bxh[c, 0])
        add(c, xm, z, high_end, bxh[c, 1])
        send(
            c,
            15,
            [(pt.at[c, xp, z, end], bxf.at[c, 0]), (pt.at[c, xm, z, end], bxf.at[c, 1])],
            x_to,
        )

    frag = frag_ref[0]
    index = lax.bitwise_and(frag, FRAGS - 1)
    rate = 0.4 + 0.6 * frag.astype(F32) / WINDOWS
    width = cw * nc // FRAGS

    def r4(c):
        chosen = index == (c * cw) // width
        inside = pl.ds((c * cw) % width, cw)
        for phase, part, far in ((14, top, rzf), (15, end, bxf)):
            arrive(c, phase)
            grad = pt[c, x, z, part, :].astype(F32)
            grad = (grad + far[c, 0].astype(F32) + far[c, 1].astype(F32)) * scale
            old = w[part, cols(c)]
            moment1 = 0.9 * m1[part, cols(c)] + 0.1 * grad
            moment2 = 0.95 * m2[part, cols(c)] + 0.05 * grad * grad
            stepped = old - 0.25 * (moment1 / (jnp.sqrt(moment2) + 1e-08) + 0.1 * old)
            mixed = 0.5 * anc_full[part, inside] + 0.5 * stepped
            nw[part, cols(c)] = jnp.where(chosen, mixed, stepped)
        copy = pltpu.make_async_copy(nw.at[:, cols(c)], nw_hbm.at[:, cols(c)], out_sem.at[c])
        copy.start()
        sent["out", c] = copy

    spans = []
    base = 0
    share = width // replicas
    for b, h in zip(bits, halves):
        size = b * share
        spans.append((base, base + h * size, base + (1 - h) * size, size))
        base = base + h * size
    own_rows = pl.ds(pl.multiple_of(base, share), share)

    def trade(k, n, src, dst):
        copy = pltpu.make_async_remote_copy(
            src_ref=src,
            dst_ref=dst,
            send_sem=osend.at[n],
            recv_sem=orecv.at[n],
            device_id={"replica": partners[k]},
            device_id_type=MESH,
        )
        copy.start()
        sent["outer", n] = copy

    def halve(k):
        _, keep, give, size = spans[k]
        trade(
            k,
            k,
            old_t.at[pl.ds(pl.multiple_of(give, share), size)],
            got.at[pl.ds(size, size)],
        )

    def halve_done(k):
        _, keep, give, size = spans[k]
        sent["outer", k].wait_recv()
        kept = pl.ds(pl.multiple_of(keep, share), size)
        old_t[kept, :] = old_t[kept, :] + got[pl.ds(size, size), :]

    def double(k):
        _, keep, give, size = spans[k]
        part = anc_t.at[pl.ds(pl.multiple_of(keep, share), size)]
        trade(k, len(bits) + k, part, part)

    def outer_begin():
        picked = w[:, pl.ds(0, width)]
        for k in range(1, FRAGS):
            picked = jnp.where(index == k, w[:, pl.ds(k * width, width)], picked)
        tall[pl.ds(0, rows), :] = picked
        tall[pl.ds(rows, LANES - rows), :] = jnp.zeros((LANES - rows, width), F32)
        old_t[...] = tall[...].T
        halve(0)

    def outer_update():
        mean = old_t[own_rows, pl.ds(0, rows)] / replicas
        anchor, moment = anc_ref[0], mom_ref[0]
        for k in range(1, FRAGS):
            anchor = jnp.where(index == k, anc_ref[k], anchor)
            moment = jnp.where(index == k, mom_ref[k], moment)
        outer = anchor - mean
        moment = 0.9 * moment + outer
        anchor = anchor - rate * (outer + 0.9 * moment)
        for k in range(FRAGS):
            na_ref[k] = jnp.where(index == k, anchor, anc_ref[k])
            nm_ref[k] = jnp.where(index == k, moment, mom_ref[k])
        anc_t[own_rows, pl.ds(0, rows)] = anchor
        anc_t[own_rows, pl.ds(rows, LANES - rows)] = jnp.zeros((share, LANES - rows), F32)

    def outer_end():
        tall[...] = anc_t[...].T
        anc_full[...] = tall[pl.ds(0, rows), :]

    def turn(k, count):
        tiles = depth // 128 // count

        def one(i, carry):
            at = pl.ds(pl.multiple_of((k * tiles + i) * 128, 128), 128)
            act_t[at, :] = act[:, at].T
            return carry

        lax.fori_loop(0, tiles, one, 0)

    last = len(bits) - 1
    loads[0].wait()
    pl.semaphore_wait(barrier, 4 + len(bits))
    a0(0)
    outer_begin()
    a1(0)
    a0(1)
    loads[1].wait()
    turn(0, 4)
    a2(0)
    a1(1)
    turn(1, 4)
    a2(1)
    a0(2)
    turn(2, 4)
    a3(0)
    turn(3, 4)
    for load in loads[2:]:
        load.wait()
    extra = []
    for k in range(last):
        extra.append(lambda k=k: (halve_done(k), halve(k + 1)))
    extra.append(lambda: (halve_done(last), outer_update(), double(last)))
    for k in range(last - 1, -1, -1):
        extra.append(lambda k=k: (sent["outer", len(bits) + k + 1].wait_recv(), double(k)))
    extra.append(lambda: (sent["outer", len(bits)].wait_recv(), outer_end()))
    for i in range(nc):
        a4(i)
        compute(i)
        if i >= 2:
            r4(i - 2)
        if i + 1 < nc:
            a3(i + 1)
        for _ in range(2):
            if extra:
                extra.pop(0)()
        if i >= 1:
            r2(i - 1)
        if i + 2 < nc:
            a1(i + 2)
            a2(i + 2)
        if i + 3 < nc:
            a0(i + 3)
        while extra and i == 1:
            extra.pop(0)()
        r1(i)
        if i >= 1:
            r3(i - 1)
    r2(nc - 1)
    r4(nc - 2)
    r3(nc - 1)
    r4(nc - 1)
    for key, copies in sent.items():
        if key[0] == "out":
            copies.wait()
        elif key[0] == "outer":
            copies.wait_send()
        else:
            for copy in copies:
                copy.wait_send()


def shards(activations, teacher, weights, first_moment, second_moment, anchor, momentum, fragment):
    tokens, depth = activations.shape[1:]
    rows, width = weights.shape[1:]
    replicas = lax.axis_size("replica")
    share = anchor.shape[2]
    whole = share * replicas
    cw = width // CHUNKS
    ra, rb = ROWS_A, rows - ROWS_A
    batch = tokens * lax.axis_size("fsdp")
    bits = replicas.bit_length() - 1
    vmem = pltpu.VMEM
    anywhere = pl.BlockSpec(memory_space=pl.ANY)
    inside = pl.BlockSpec(memory_space=pltpu.VMEM)
    new_w, new_a, new_m = pl.pallas_call(
        functools.partial(kernel, batch),
        out_shape=(
            jax.ShapeDtypeStruct((rows, width), F32),
            jax.ShapeDtypeStruct((FRAGS, share, rows), F32),
            jax.ShapeDtypeStruct((FRAGS, share, rows), F32),
        ),
        in_specs=[pl.BlockSpec(memory_space=pltpu.SMEM)] + [anywhere] * 5 + [inside] * 2,
        out_specs=(anywhere, inside, inside),
        scratch_shapes=[
            vmem((tokens, depth), BF16),
            vmem((depth, tokens), BF16),
            vmem((tokens, width), BF16),
            vmem((rows, width), F32),
            vmem((rows, width), F32),
            vmem((rows, width), F32),
            vmem((rows, width), F32),
            vmem((CHUNKS, SIDE, SIDE, rows, cw), BF16),
            vmem((CHUNKS, SIDE, SIDE, rows, cw), BF16),
            vmem((tokens, cw), BF16),
            vmem((8, 128), F32),
            vmem((CHUNKS, 2, SIDE, ra // 2, cw), BF16),
            vmem((CHUNKS, 2, SIDE, ra, cw), BF16),
            vmem((CHUNKS, 2, ra // 2, cw), BF16),
            vmem((CHUNKS, 2, ra, cw), BF16),
            vmem((CHUNKS, 2, SIDE, rb // 2, cw), BF16),
            vmem((CHUNKS, 2, SIDE, rb, cw), BF16),
            vmem((CHUNKS, 2, rb // 2, cw), BF16),
            vmem((CHUNKS, 2, rb, cw), BF16),
            vmem((LANES, whole), F32),
            vmem((whole, LANES), F32),
            vmem((whole, LANES), F32),
            vmem((rows, whole), F32),
            vmem((whole, LANES), F32),
            pltpu.SemaphoreType.DMA((5,)),
            pltpu.SemaphoreType.DMA((CHUNKS,)),
            pltpu.SemaphoreType.DMA((CHUNKS, 16, 2)),
            pltpu.SemaphoreType.DMA((CHUNKS, 16, 2)),
            pltpu.SemaphoreType.DMA((2 * bits,)),
            pltpu.SemaphoreType.DMA((2 * bits,)),
        ],
        compiler_params=pltpu.CompilerParams(
            collective_id=0, has_side_effects=True, vmem_limit_bytes=60 * 2**20
        ),
    )(
        fragment,
        activations[0],
        teacher[0],
        weights[0],
        first_moment[0],
        second_moment[0],
        jnp.swapaxes(anchor, 1, 2),
        jnp.swapaxes(momentum, 1, 2),
    )
    return (new_w[None], jnp.swapaxes(new_a, 1, 2), jnp.swapaxes(new_m, 1, 2))


def solution(mesh):
    in_specs = (
        P("replica", "fsdp", None),
        P("replica", "fsdp", None),
        P("replica", "fsdp", None),
        P("replica", "fsdp", None),
        P("replica", "fsdp", None),
        P(None, "fsdp", "replica"),
        P(None, "fsdp", "replica"),
        P(),
    )
    out_specs = (P("replica", "fsdp", None), P(None, "fsdp", "replica"), P(None, "fsdp", "replica"))
    return jax.shard_map(shards, mesh=mesh, in_specs=in_specs, out_specs=out_specs, check_vma=False)
```

time: 329 us -> 184 us (0.56)
  waiting for transfers between devices: 209 us -> 0 us
  Pallas kernels: 0 us -> 179 us
  blocking collectives: 44.5 us -> 0 us
  local copies, waits for them, and re-layouts: 28.7 us -> 3.74 us
  matrix products: 23.5 us -> 0 us
  between operations: 16.2 us -> 1.31 us
  other arithmetic: 4.87 us -> 0 us
    pallas_call x0 -> x1, Pallas kernels: none -> 179 us  [shards(): pl.pallas_call(functools.partial(kernel, batch), out_shape=(jax.ShapeDtyp...]
    all_gather x1 -> x0, waiting for transfers between devices: 128 us -> none  [shards(): lax.all_gather(low, 'fsdp', axis=0, tiled=True)]
    unnamed x4 -> x0, waiting for transfers between devices: 81.3 us -> none
    all_gather x2 -> x0, blocking collectives: 44.5 us -> none  [the longest x1 23.5 us: shards(): lax.all_gather(own_anchor.astype(jnp.bfloat16), 'replica', axis=1, tiled=...]
    dot_general x2 -> x0, matrix products: 23.5 us -> none  [the longest x1 12.6 us: shards(): lax.dot_general(columns, error, (((0,), (0,)), ((), ())), preferred_eleme...]
    unnamed x15 -> x7, local copies, waits for them, and re-layouts: 25.6 us -> 3.74 us
  transfers between devices with their start and end apart: 3 -> 0, of which waited for: 2 -> 0; matrix products, arithmetic and copies ran while one was open for 13% -> 0% of each run, Pallas kernels for 0% -> 0%
where the time goes in v1:
time: 184 us
  Pallas kernels  179 us (97%)
  local copies, waits for them, and re-layouts  3.74 us (2%)
    pallas_call x1, Pallas kernels, shards(): pl.pallas_call(functools.partial(kernel, batch), out_shape=(jax.ShapeDtyp...  179 us
    unnamed x7, local copies, waits for them, and re-layouts  3.74 us

profile of v1, /device:TPU:32, one launch (start us, length us, event | category | flops | bytes accessed | tf_op | source)
XLA Modules:
  0.0 184.3 jit_solution(13285943363424807154)
XLA Ops:
  1.3 179.2 %shard_map.103 = (f32[288,1024]{1,0:T(8,128)}, f32[4,16,288]{2,1,0:T(8,128)}, f32[4,16,288]{2,1,0:T(8,128)}) custom-call(s32[1]{0:T(128)S(6)} %copy.14.frag_ref, bf16[640,4608]{1,0:T(8,128)(2,1)} %bitcast.10, bf16[640,1024]{1,0:T(8,128)(2,1)} %bitcast.11, f32[288,1024]{1,0:T(8,128)} %bitcast.13, f32[288,1024]{1,0:T(8,128)} %bitcast.14, ...), custom_call_target="tpu_custom_call" | custom-call | tf_op jit(solution)/shard_map/pallas_call | solution.py:462
  180.5 0.0 copy-start.1
  180.5 0.0 copy-start
  180.5 2.4 %copy.15 = f32[1,288,1024]{2,1,0:T(8,128)} copy(f32[1,288,1024]{2,1,0:T(8,128)} %bitcast.12) | data formatting | bytes 2359296
  183.0 0.0 copy-done.1
  183.0 0.6 copy.16
  183.6 0.0 copy-done
  183.6 0.6 copy.17
Async XLA Ops:
  180.5 2.5 %copy-start.1 = (f32[4,16,288]{2,1,0:T(8,128)S(1)}, f32[4,16,288]{2,1,0:T(8,128)}, u32[]{:S(2)}) copy-start(f32[4,16,288]{2,1,0:T(8,128)} %get-tuple-element.7) | copy-start | bytes 221188
  180.5 3.1 %copy-start = (f32[4,16,288]{2,1,0:T(8,128)S(1)}, f32[4,16,288]{2,1,0:T(8,128)}, u32[]{:S(2)}) copy-start(f32[4,16,288]{2,1,0:T(8,128)} %get-tuple-element.8) | copy-start | bytes 221188

commit v2 on v1

--- a/solution.py
+++ b/solution.py
@@ -14,9 +14,38 @@
 CHUNKS = 4
 ROWS_A = 224
 LANES = 384
+PHASES = 32
+SPLIT_GATHER = (0, 1)
+SPLIT_SCATTER = (2, 3)
+ORDER = (
+    ("a0", 1), ("a1x", 1), ("o", 0), ("a0", 0), ("a0", 2), ("o", 0), ("a1z", 1), ("o", 0), ("a3x0", 0),
+    ("a1x", 2), ("a1x", 0), ("T", 0), ("a1z", 0), ("a2z", 0), ("a2x", 1), ("o", 0), ("a2x", 0), ("T", 0),
+    ("T", 0), ("a3x1", 0), ("a1z", 2), ("a3x2", 1), ("a3z", 0), ("o", 0), ("a0", 3), ("a3x1", 1), ("o", 0),
+    ("a3x2", 0), ("a2x", 2), ("a4", 0), ("a3x0", 1), ("a2z", 1), ("T", 0), ("a2z", 2), ("C", 0), ("a3z", 1),
+    ("a3x", 2), ("r1x", 0), ("r1z", 0), ("o", 0), ("o", 0), ("a1z", 3), ("a1x", 3), ("a4", 1), ("a3z", 2),
+    ("C", 1), ("a2x", 3), ("a2z", 3), ("r1z", 1), ("a4", 2), ("r1x", 1), ("C", 2), ("a3z", 3), ("r1z", 2),
+    ("a3x", 3), ("r2z", 0), ("r2z", 1), ("r2x", 0), ("r1x0", 2), ("r1x1", 2), ("r3z", 1), ("r3z", 0),
+    ("a4", 3), ("C", 3), ("r2x", 1), ("r2z1", 2), ("o", 0), ("r1x0", 3), ("r2x", 2), ("r2z0", 2), ("r1z", 3),
+    ("r1x1", 3), ("r3x", 0), ("r2z0", 3), ("r2z1", 3), ("r3z", 2), ("r4", 0), ("r1x2", 3), ("r2x", 3),
+    ("r1x2", 2), ("r3z", 3), ("r3x", 1), ("r3x", 3), ("r3x", 2), ("r2z2", 2), ("r4", 1), ("r4", 2),
+    ("r2z2", 3), ("r4", 3),
+)
 MESH = pl.DeviceIdType.MESH
 F32 = jnp.float32
 BF16 = jnp.bfloat16
+
+
+def exchange_bits(replicas):
+    bits = [1 << k for k in range(replicas.bit_length() - 1)]
+    return bits[:1] + bits[2:] + bits[1:2]
+
+
+def place(replica, replicas):
+    at, size = 0, replicas // 2
+    for bit in exchange_bits(replicas):
+        at += size if replica & bit else 0
+        size //= 2
+    return at
 
 
 def kernel(
@@ -42,7 +71,6 @@
     wf,
     pt,
     err,
-    acc,
     rxh,
     rxf,
     rzh,
@@ -78,11 +106,7 @@
     zp, zm, z2 = (lax.rem(z + k, SIDE) for k in (1, 3, 2))
     x_to = [xp * SIDE + z, xm * SIDE + z]
     z_to = [x * SIDE + zp, x * SIDE + zm]
-    bits = []
-    step = replicas // 2
-    while step:
-        bits.append(step)
-        step //= 2
+    bits = exchange_bits(replicas)
     halves = [lax.rem(lax.div(rep, b), 2) for b in bits]
     partners = [rep + b - 2 * b * h for b, h in zip(bits, halves)]
 
@@ -138,32 +162,57 @@
         wf[c, x, z] = w[:, cols(c)].astype(BF16)
         own = wf.at[c, x, z, top]
         send(c, 0, same(own, own), z_to)
+        if c in SPLIT_GATHER:
+            send(c, 4, same(own, own), x_to)
         own = wf.at[c, x, z, end]
         send(c, 1, same(own, own), x_to)
 
-    def a1(c):
+    def a1z(c):
         arrive(c, 0)
         send(c, 2, same(wf.at[c, x, zm, low_half], wf.at[c, x, zp, high_half]), z_to)
+        if c in SPLIT_GATHER:
+            for phase, k in ((16, zm), (17, zp)):
+                far = wf.at[c, x, k, top]
+                send(c, phase, same(far, far), x_to)
+
+    def a1x(c):
         arrive(c, 1)
         send(c, 3, same(wf.at[c, xm, z, low_end], wf.at[c, xp, z, high_end]), x_to)
 
-    def a2(c):
+    def a2x(c):
         arrive(c, 2)
-        own = wf.at[c, x, every, top]
-        send(c, 4, same(own, own), x_to)
+        far = wf.at[c, x, z2, top] if c in SPLIT_GATHER else wf.at[c, x, every, top]
+        send(c, 18 if c in SPLIT_GATHER else 4, same(far, far), x_to)
+
+    def a2z(c):
         arrive(c, 3)
         own = wf.at[c, every, z, end]
         send(c, 5, same(own, own), z_to)
 
-    def a3(c):
-        arrive(c, 4)
-        send(c, 6, same(wf.at[c, xm, every, low_half], wf.at[c, xp, every, high_half]), x_to)
+    def pass_on(c, phase, then, k):
+        arrive(c, phase)
+        send(c, then, same(wf.at[c, xm, k, low_half], wf.at[c, xp, k, high_half]), x_to)
+
+    def a3x(c):
+        pass_on(c, 4, 6, every)
+
+    def a3x0(c):
+        pass_on(c, 4, 6, z)
+
+    def a3x1(c):
+        pass_on(c, 16, 19, zm)
+        pass_on(c, 17, 20, zp)
+
+    def a3x2(c):
+        pass_on(c, 18, 21, z2)
+
+    def a3z(c):
         arrive(c, 5)
         send(c, 7, same(wf.at[c, every, zm, low_end], wf.at[c, every, zp, high_end]), z_to)
 
     def a4(c):
-        arrive(c, 6)
-        arrive(c, 7)
+        for phase in (6, 19, 20, 21, 7) if c in SPLIT_GATHER else (6, 7):
+            arrive(c, phase)
 
     def compute(c):
         total = None
@@ -184,15 +233,10 @@
             )
             pt[c, g] = part.astype(BF16).reshape(SIDE, rows, cw)
             if g is x2:
-                send(
-                    c,
-                    8,
-                    [
-                        (pt.at[c, x2, every, low_half], rxh.at[c, 0]),
-                        (pt.at[c, x2, every, high_half], rxh.at[c, 1]),
-                    ],
-                    x_to,
-                )
+                for phase, k in by_shard(c, 8):
+                    low = (pt.at[c, x2, k, low_half], rxh.at[c, 0, k])
+                    high = (pt.at[c, x2, k, high_half], rxh.at[c, 1, k])
+                    send(c, phase, [low, high], x_to)
         send(
             c,
             9,
@@ -203,26 +247,44 @@
             z_to,
         )
 
+    def by_shard(c, first):
+        if c not in SPLIT_SCATTER:
+            return [(first, every)]
+        base = 22 if first == 8 else 25
+        return [(first, z2), (base, zm), (base + 1, zp), (base + 2, z)]
+
     def add(c, i, j, part, *terms):
         total = pt[c, i, j, part, :].astype(F32)
         for term in terms:
             total = total + term.astype(F32)
         pt[c, i, j, part, :] = total.astype(BF16)
 
-    def r1(c):
-        arrive(c, 8)
-        for k in range(SIDE):
-            add(c, xp, k, low_half, rxh[c, 0, k])
-            add(c, xm, k, high_half, rxh[c, 1, k])
-        send(
-            c,
-            10,
-            [
-                (pt.at[c, xp, every, top], rxf.at[c, 0]),
-                (pt.at[c, xm, every, top], rxf.at[c, 1]),
-            ],
-            x_to,
-        )
+    def first_sum(c, groups):
+        for (phase, k), (then, _) in groups:
+            arrive(c, phase)
+            for j in range(SIDE) if k is every else (k,):
+                add(c, xp, j, low_half, rxh[c, 0, j])
+                add(c, xm, j, high_half, rxh[c, 1, j])
+            right = (pt.at[c, xp, k, top], rxf.at[c, 0, k])
+            left = (pt.at[c, xm, k, top], rxf.at[c, 1, k])
+            send(c, then, [right, left], x_to)
+
+    def groups_of(c):
+        return list(zip(by_shard(c, 8), by_shard(c, 10)))
+
+    def r1x(c):
+        first_sum(c, groups_of(c))
+
+    def r1x0(c):
+        first_sum(c, groups_of(c)[:1])
+
+    def r1x1(c):
+        first_sum(c, groups_of(c)[1:3])
+
+    def r1x2(c):
+        first_sum(c, groups_of(c)[3:])
+
+    def r1z(c):
         arrive(c, 9)
         for k in range(SIDE):
             add(c, k, zp, low_end, bzh[c, 0, k])
@@ -237,19 +299,32 @@
             z_to,
         )
 
-    def r2(c):
-        arrive(c, 10)
-        for k in range(SIDE):
-            add(c, x, k, top, rxf[c, 0, k], rxf[c, 1, k])
-        send(
-            c,
-            12,
-            [
-                (pt.at[c, x, z2, low_half], rzh.at[c, 0]),
-                (pt.at[c, x, z2, high_half], rzh.at[c, 1]),
-            ],
-            z_to,
-        )
+    def second_sum(c, groups):
+        for phase, k in groups:
+            arrive(c, phase)
+            for j in range(SIDE) if k is every else (k,):
+                add(c, x, j, top, rxf[c, 0, j], rxf[c, 1, j])
+
+    def send_far(c):
+        low = (pt.at[c, x, z2, low_half], rzh.at[c, 0])
+        high = (pt.at[c, x, z2, high_half], rzh.at[c, 1])
+        send(c, 12, [low, high], z_to)
+
+    def r2z(c):
+        second_sum(c, by_shard(c, 10))
+        send_far(c)
+
+    def r2z0(c):
+        second_sum(c, by_shard(c, 10)[:1])
+        send_far(c)
+
+    def r2z1(c):
+        second_sum(c, by_shard(c, 10)[1:3])
+
+    def r2z2(c):
+        second_sum(c, by_shard(c, 10)[3:])
+
+    def r2x(c):
         arrive(c, 11)
         for k in range(SIDE):
             add(c, k, z, end, bzf[c, 0, k], bzf[c, 1, k])
@@ -263,7 +338,7 @@
             x_to,
         )
 
-    def r3(c):
+    def r3z(c):
         arrive(c, 12)
         add(c, x, zp, low_half, rzh[c, 0])
         add(c, x, zm, high_half, rzh[c, 1])
@@ -273,6 +348,8 @@
             [(pt.at[c, x, zp, top], rzf.at[c, 0]), (pt.at[c, x, zm, top], rzf.at[c, 1])],
             z_to,
         )
+
+    def r3x(c):
         arrive(c, 13)
         add(c, xp, z, low_end, bxh[c, 0])
         add(c, xm, z, high_end, bxh[c, 1])
@@ -308,8 +385,8 @@
     spans = []
     base = 0
     share = width // replicas
-    for b, h in zip(bits, halves):
-        size = b * share
+    for k, h in enumerate(halves):
+        size = width >> (k + 1)
         spans.append((base, base + h * size, base + (1 - h) * size, size))
         base = base + h * size
     own_rows = pl.ds(pl.multiple_of(base, share), share)
@@ -352,7 +429,10 @@
             picked = jnp.where(index == k, w[:, pl.ds(k * width, width)], picked)
         tall[pl.ds(0, rows), :] = picked
         tall[pl.ds(rows, LANES - rows), :] = jnp.zeros((LANES - rows, width), F32)
-        old_t[...] = tall[...].T
+        anc_t[...] = tall[...].T
+        for r in range(replicas):
+            at = pl.ds(place(r, replicas) * share, share)
+            old_t[at, :] = anc_t[pl.ds(r * share, share), :]
         halve(0)
 
     def outer_update():
@@ -371,7 +451,10 @@
         anc_t[own_rows, pl.ds(rows, LANES - rows)] = jnp.zeros((share, LANES - rows), F32)
 
     def outer_end():
-        tall[...] = anc_t[...].T
+        for r in range(replicas):
+            at = pl.ds(place(r, replicas) * share, share)
+            got[pl.ds(r * share, share), :] = anc_t[at, :]
+        tall[...] = got[...].T
         anc_full[...] = tall[pl.ds(0, rows), :]
 
     def turn(k, count):
@@ -384,58 +467,50 @@
 
         lax.fori_loop(0, tiles, one, 0)
 
-    last = len(bits) - 1
+    steps = len(bits)
+    outer = [outer_begin]
+    for k in range(1, steps):
+        outer.append(lambda k=k: (halve_done(k - 1), halve(k)))
+    outer.append(lambda: (halve_done(steps - 1), outer_update(), double(steps - 1)))
+    for k in range(steps - 1, 0, -1):
+        outer.append(lambda k=k: (sent["outer", steps + k].wait_recv(), double(k - 1)))
+    outer.append(lambda: (sent["outer", steps].wait_recv(), outer_end()))
+
+    events = {
+        "a0": a0,
+        "a1z": a1z,
+        "a1x": a1x,
+        "a2x": a2x,
+        "a2z": a2z,
+        "a3x": a3x,
+        "a3x0": a3x0,
+        "a3x1": a3x1,
+        "a3x2": a3x2,
+        "a3z": a3z,
+        "a4": a4,
+        "C": compute,
+        "r1x": r1x,
+        "r1x0": r1x0,
+        "r1x1": r1x1,
+        "r1x2": r1x2,
+        "r1z": r1z,
+        "r2z": r2z,
+        "r2z0": r2z0,
+        "r2z1": r2z1,
+        "r2z2": r2z2,
+        "r2x": r2x,
+        "r3z": r3z,
+        "r3x": r3x,
+        "r4": r4,
+        "T": lambda c: turns.pop(0)(),
+        "o": lambda c: outer.pop(0)(),
+    }
+    turns = [lambda: (loads[1].wait(), turn(0, 4)), lambda: turn(1, 4), lambda: turn(2, 4)]
+    turns.append(lambda: (turn(3, 4), [load.wait() for load in loads[2:]]))
     loads[0].wait()
     pl.semaphore_wait(barrier, 4 + len(bits))
-    a0(0)
-    outer_begin()
-    a1(0)
-    a0(1)
-    loads[1].wait()
-    turn(0, 4)
-    a2(0)
-    a1(1)
-    turn(1, 4)
-    a2(1)
-    a0(2)
-    turn(2, 4)
-    a3(0)
-    turn(3, 4)
-    for load in loads[2:]:
-        load.wait()
-    extra = []
-    for k in range(last):
-        extra.append(lambda k=k: (halve_done(k), halve(k + 1)))
-    extra.append(lambda: (halve_done(last), outer_update(), double(last)))
-    for k in range(last - 1, -1, -1):
-        extra.append(lambda k=k: (sent["outer", len(bits) + k + 1].wait_recv(), double(k)))
-    extra.append(lambda: (sent["outer", len(bits)].wait_recv(), outer_end()))
-    for i in range(nc):
-        a4(i)
-        compute(i)
-        if i >= 2:
-            r4(i - 2)
-        if i + 1 < nc:
-            a3(i + 1)
-        for _ in range(2):
-            if extra:
-                extra.pop(0)()
-        if i >= 1:
-            r2(i - 1)
-        if i + 2 < nc:
-            a1(i + 2)
-            a2(i + 2)
-        if i + 3 < nc:
-            a0(i + 3)
-        while extra and i == 1:
-            extra.pop(0)()
-        r1(i)
-        if i >= 1:
-            r3(i - 1)
-    r2(nc - 1)
-    r4(nc - 2)
-    r3(nc - 1)
-    r4(nc - 1)
+    for event, c in ORDER:
+        events[event](c)
     for key, copies in sent.items():
         if key[0] == "out":
             copies.wait()
@@ -479,7 +554,6 @@
             vmem((CHUNKS, SIDE, SIDE, rows, cw), BF16),
             vmem((CHUNKS, SIDE, SIDE, rows, cw), BF16),
             vmem((tokens, cw), BF16),
-            vmem((8, 128), F32),
             vmem((CHUNKS, 2, SIDE, ra // 2, cw), BF16),
             vmem((CHUNKS, 2, SIDE, ra, cw), BF16),
             vmem((CHUNKS, 2, ra // 2, cw), BF16),
@@ -495,8 +569,8 @@
             vmem((whole, LANES), F32),
             pltpu.SemaphoreType.DMA((5,)),
             pltpu.SemaphoreType.DMA((CHUNKS,)),
-            pltpu.SemaphoreType.DMA((CHUNKS, 16, 2)),
-            pltpu.SemaphoreType.DMA((CHUNKS, 16, 2)),
+            pltpu.SemaphoreType.DMA((CHUNKS, PHASES, 2)),
+            pltpu.SemaphoreType.DMA((CHUNKS, PHASES, 2)),
             pltpu.SemaphoreType.DMA((2 * bits,)),
             pltpu.SemaphoreType.DMA((2 * bits,)),
         ],

time: 184 us -> 161 us (0.88); the launches traced: 184 us -> 159 us
  Pallas kernels: 179 us -> 154 us
    pallas_call x1, Pallas kernels: 179 us -> 154 us  [shards(): pl.pallas_call(functools.partial(kernel, batch), out_shape=(jax.ShapeDtyp...]
where the time goes in v2:
time: 161 us; the launch traced here: 159 us
  Pallas kernels  154 us (96%)
  local copies, waits for them, and re-layouts  3.74 us (2%)
    pallas_call x1, Pallas kernels, shards(): pl.pallas_call(functools.partial(kernel, batch), out_shape=(jax.ShapeDtyp...  154 us
    unnamed x7, local copies, waits for them, and re-layouts  3.74 us

profile of v2, /device:TPU:32, one launch (start us, length us, event | category | flops | bytes accessed | tf_op | source)
XLA Modules:
  0.0 158.5 jit_solution(13362548739336351341)
XLA Ops:
  1.3 153.5 %shard_map.103 = (f32[288,1024]{1,0:T(8,128)}, f32[4,16,288]{2,1,0:T(8,128)}, f32[4,16,288]{2,1,0:T(8,128)}) custom-call(s32[1]{0:T(128)S(6)} %copy.14.frag_ref, bf16[640,4608]{1,0:T(8,128)(2,1)} %bitcast.10, bf16[640,1024]{1,0:T(8,128)(2,1)} %bitcast.11, f32[288,1024]{1,0:T(8,128)} %bitcast.13, f32[288,1024]{1,0:T(8,128)} %bitcast.14, ...), custom_call_target="tpu_custom_call" | custom-call | tf_op jit(solution)/shard_map/pallas_call | solution.py:537
  154.8 0.0 copy-start.1
  154.8 0.0 copy-start
  154.8 2.4 %copy.15 = f32[1,288,1024]{2,1,0:T(8,128)} copy(f32[1,288,1024]{2,1,0:T(8,128)} %bitcast.12) | data formatting | bytes 2359296
  157.3 0.0 copy-done.1
  157.3 0.6 copy.16
  157.9 0.0 copy-done
  157.9 0.6 copy.17
Async XLA Ops:
  154.8 2.5 %copy-start.1 = (f32[4,16,288]{2,1,0:T(8,128)S(1)}, f32[4,16,288]{2,1,0:T(8,128)}, u32[]{:S(2)}) copy-start(f32[4,16,288]{2,1,0:T(8,128)} %get-tuple-element.7) | copy-start | bytes 221188
  154.8 3.1 %copy-start = (f32[4,16,288]{2,1,0:T(8,128)S(1)}, f32[4,16,288]{2,1,0:T(8,128)}, u32[]{:S(2)}) copy-start(f32[4,16,288]{2,1,0:T(8,128)} %get-tuple-element.8) | copy-start | bytes 221188

commit v3 on v2

--- a/solution.py
+++ b/solution.py
@@ -15,20 +15,20 @@
 ROWS_A = 224
 LANES = 384
 PHASES = 32
-SPLIT_GATHER = (0, 1)
-SPLIT_SCATTER = (2, 3)
+SPLIT_GATHER = (0, 1, 2)
+SPLIT_SCATTER = (1, 2, 3)
 ORDER = (
-    ("a0", 1), ("a1x", 1), ("o", 0), ("a0", 0), ("a0", 2), ("o", 0), ("a1z", 1), ("o", 0), ("a3x0", 0),
-    ("a1x", 2), ("a1x", 0), ("T", 0), ("a1z", 0), ("a2z", 0), ("a2x", 1), ("o", 0), ("a2x", 0), ("T", 0),
-    ("T", 0), ("a3x1", 0), ("a1z", 2), ("a3x2", 1), ("a3z", 0), ("o", 0), ("a0", 3), ("a3x1", 1), ("o", 0),
-    ("a3x2", 0), ("a2x", 2), ("a4", 0), ("a3x0", 1), ("a2z", 1), ("T", 0), ("a2z", 2), ("C", 0), ("a3z", 1),
-    ("a3x", 2), ("r1x", 0), ("r1z", 0), ("o", 0), ("o", 0), ("a1z", 3), ("a1x", 3), ("a4", 1), ("a3z", 2),
-    ("C", 1), ("a2x", 3), ("a2z", 3), ("r1z", 1), ("a4", 2), ("r1x", 1), ("C", 2), ("a3z", 3), ("r1z", 2),
-    ("a3x", 3), ("r2z", 0), ("r2z", 1), ("r2x", 0), ("r1x0", 2), ("r1x1", 2), ("r3z", 1), ("r3z", 0),
-    ("a4", 3), ("C", 3), ("r2x", 1), ("r2z1", 2), ("o", 0), ("r1x0", 3), ("r2x", 2), ("r2z0", 2), ("r1z", 3),
-    ("r1x1", 3), ("r3x", 0), ("r2z0", 3), ("r2z1", 3), ("r3z", 2), ("r4", 0), ("r1x2", 3), ("r2x", 3),
-    ("r1x2", 2), ("r3z", 3), ("r3x", 1), ("r3x", 3), ("r3x", 2), ("r2z2", 2), ("r4", 1), ("r4", 2),
-    ("r2z2", 3), ("r4", 3),
+    ("a0", 0), ("a0", 2), ("a0", 1), ("a1x", 0), ("a1z", 0), ("a1x", 2), ("a1z", 2), ("a1z", 1), ("a1x", 1),
+    ("a0", 3), ("T", 0), ("T", 0), ("a3x1", 0), ("a2x", 1), ("T", 0), ("a2x", 0), ("a2x", 2), ("a3x0", 0),
+    ("a2z", 0), ("o", 0), ("a1z", 3), ("a3x0", 1), ("a2z", 1), ("a3x1", 1), ("a3x2", 0), ("a1x", 3),
+    ("a3z", 0), ("a3z", 1), ("o", 0), ("a3x2", 2), ("a3x2", 1), ("a3x1", 2), ("T", 0), ("a2z", 2), ("o", 0),
+    ("a3x0", 2), ("a2x", 3), ("a2z", 3), ("a4", 1), ("a4", 0), ("C", 0), ("a3z", 2), ("o", 0), ("C", 1),
+    ("r1z", 0), ("r1x0", 1), ("a3x", 3), ("a4", 2), ("a3z", 3), ("C", 2), ("o", 0), ("r1x1", 1), ("r2z0", 1),
+    ("r1z", 1), ("a4", 3), ("C", 3), ("r1x", 0), ("r1z", 2), ("r1x0", 2), ("r2z1", 1), ("r1x0", 3),
+    ("r2x", 1), ("o", 0), ("r1x1", 3), ("r1z", 3), ("r3z", 1), ("o", 0), ("r2z0", 2), ("o", 0), ("r1x1", 2),
+    ("r2z0", 3), ("r1x2", 1), ("r2x", 0), ("r2z", 0), ("r2z1", 3), ("r3z", 3), ("r2x", 2), ("r3z", 0),
+    ("r2z1", 2), ("r1x2", 3), ("r3x", 0), ("r3z", 2), ("r2x", 3), ("r3x", 1), ("r2z2", 1), ("r1x2", 2),
+    ("r3x", 3), ("r3x", 2), ("o", 0), ("r4", 0), ("r2z2", 3), ("r4", 1), ("r2z2", 2), ("r4", 3), ("r4", 2),
 )
 MESH = pl.DeviceIdType.MESH
 F32 = jnp.float32
@@ -56,8 +56,8 @@
     w_hbm,
     m1_hbm,
     m2_hbm,
-    anc_ref,
-    mom_ref,
+    anc_hbm,
+    mom_hbm,
     nw_hbm,
     na_ref,
     nm_ref,
@@ -79,6 +79,8 @@
     bzf,
     bxh,
     bxf,
+    anc_ref,
+    mom_ref,
     tall,
     old_t,
     anc_t,
@@ -119,7 +121,15 @@
     loads = [
         pltpu.make_async_copy(src, dst, in_sem.at[k])
         for k, (src, dst) in enumerate(
-            [(w_hbm, w), (act_hbm, act), (tgt_hbm, tgt), (m1_hbm, m1), (m2_hbm, m2)]
+            [
+                (w_hbm, w),
+                (act_hbm, act),
+                (tgt_hbm, tgt),
+                (m1_hbm, m1),
+                (m2_hbm, m2),
+                (anc_hbm, anc_ref),
+                (mom_hbm, mom_ref),
+            ]
         )
     ]
     for load in loads:
@@ -162,10 +172,10 @@
         wf[c, x, z] = w[:, cols(c)].astype(BF16)
         own = wf.at[c, x, z, top]
         send(c, 0, same(own, own), z_to)
+        short = wf.at[c, x, z, end]
+        send(c, 1, same(short, short), x_to)
         if c in SPLIT_GATHER:
             send(c, 4, same(own, own), x_to)
-        own = wf.at[c, x, z, end]
-        send(c, 1, same(own, own), x_to)
 
     def a1z(c):
         arrive(c, 0)
@@ -541,7 +551,7 @@
             jax.ShapeDtypeStruct((FRAGS, share, rows), F32),
             jax.ShapeDtypeStruct((FRAGS, share, rows), F32),
         ),
-        in_specs=[pl.BlockSpec(memory_space=pltpu.SMEM)] + [anywhere] * 5 + [inside] * 2,
+        in_specs=[pl.BlockSpec(memory_space=pltpu.SMEM)] + [anywhere] * 7,
         out_specs=(anywhere, inside, inside),
         scratch_shapes=[
             vmem((tokens, depth), BF16),
@@ -562,12 +572,14 @@
             vmem((CHUNKS, 2, SIDE, rb, cw), BF16),
             vmem((CHUNKS, 2, rb // 2, cw), BF16),
             vmem((CHUNKS, 2, rb, cw), BF16),
+            vmem((FRAGS, share, rows), F32),
+            vmem((FRAGS, share, rows), F32),
             vmem((LANES, whole), F32),
             vmem((whole, LANES), F32),
             vmem((whole, LANES), F32),
             vmem((rows, whole), F32),
             vmem((whole, LANES), F32),
-            pltpu.SemaphoreType.DMA((5,)),
+            pltpu.SemaphoreType.DMA((7,)),
             pltpu.SemaphoreType.DMA((CHUNKS,)),
             pltpu.SemaphoreType.DMA((CHUNKS, PHASES, 2)),
             pltpu.SemaphoreType.DMA((CHUNKS, PHASES, 2)),

time: 161 us -> 154 us (0.957)
  Pallas kernels: 154 us -> 146 us
    pallas_call x1, Pallas kernels: 154 us -> 146 us  [shards(): pl.pallas_call(functools.partial(kernel, batch), out_shape=(jax.ShapeDtyp...]
where the time goes in v3:
time: 154 us; the launch traced here: 151 us
  Pallas kernels  146 us (95%)
  local copies, waits for them, and re-layouts  3.74 us (2%)
    pallas_call x1, Pallas kernels, shards(): pl.pallas_call(functools.partial(kernel, batch), out_shape=(jax.ShapeDtyp...  146 us
    unnamed x7, local copies, waits for them, and re-layouts  3.74 us

profile of v3, /device:TPU:32, one launch (start us, length us, event | category | flops | bytes accessed | tf_op | source)
XLA Modules:
  0.0 151.2 jit_solution(6747379656832408662)
XLA Ops:
  1.3 146.2 %shard_map.103 = (f32[288,1024]{1,0:T(8,128)}, f32[4,16,288]{2,1,0:T(8,128)}, f32[4,16,288]{2,1,0:T(8,128)}) custom-call(s32[1]{0:T(128)S(6)} %copy.14.frag_ref, bf16[640,4608]{1,0:T(8,128)(2,1)} %bitcast.10, bf16[640,1024]{1,0:T(8,128)(2,1)} %bitcast.11, f32[288,1024]{1,0:T(8,128)} %bitcast.13, f32[288,1024]{1,0:T(8,128)} %bitcast.14, ...), custom_call_target="tpu_custom_call" | custom-call | tf_op jit(solution)/shard_map/pallas_call | solution.py:547
  147.5 0.0 copy-start.1
  147.5 0.0 copy-start
  147.5 2.4 %copy.15 = f32[1,288,1024]{2,1,0:T(8,128)} copy(f32[1,288,1024]{2,1,0:T(8,128)} %bitcast.12) | data formatting | bytes 2359296
  149.9 0.0 copy-done.1
  149.9 0.6 copy.16
  150.6 0.0 copy-done
  150.6 0.6 copy.17
Async XLA Ops:
  147.5 2.5 %copy-start.1 = (f32[4,16,288]{2,1,0:T(8,128)S(1)}, f32[4,16,288]{2,1,0:T(8,128)}, u32[]{:S(2)}) copy-start(f32[4,16,288]{2,1,0:T(8,128)} %get-tuple-element.7) | copy-start | bytes 221188
  147.5 3.1 %copy-start = (f32[4,16,288]{2,1,0:T(8,128)S(1)}, f32[4,16,288]{2,1,0:T(8,128)}, u32[]{:S(2)}) copy-start(f32[4,16,288]{2,1,0:T(8,128)} %get-tuple-element.8) | copy-start | bytes 221188

commit v4 on v3

--- a/solution.py
+++ b/solution.py
@@ -14,7 +14,6 @@
 CHUNKS = 4
 ROWS_A = 224
 LANES = 384
-PHASES = 32
 SPLIT_GATHER = (0, 1, 2)
 SPLIT_SCATTER = (1, 2, 3)
 ORDER = (
@@ -30,6 +29,9 @@
     ("r2z1", 2), ("r1x2", 3), ("r3x", 0), ("r3z", 2), ("r2x", 3), ("r3x", 1), ("r2z2", 1), ("r1x2", 2),
     ("r3x", 3), ("r3x", 2), ("o", 0), ("r4", 0), ("r2z2", 3), ("r4", 1), ("r2z2", 2), ("r4", 3), ("r4", 2),
 )
+SHORT = (1, 3, 5, 7, 9, 11, 13, 15)
+FULL = (0, 1, 4, 5, 10, 11, 14, 15, 16, 17, 18, 25, 26, 27)
+KINDS = (0, 1, 0, 1, 2, 3, 2, 3, 4, 5, 4, 5, 6, 7, 6, 7) + (2,) * 6 + (4,) * 6
 MESH = pl.DeviceIdType.MESH
 F32 = jnp.float32
 BF16 = jnp.bfloat16
@@ -138,29 +140,37 @@
     top, low_half, high_half = pl.ds(0, ra), pl.ds(0, ha), pl.ds(ha, ha)
     end, low_end, high_end = pl.ds(ra, rb), pl.ds(ra, hb), pl.ds(ra + hb, hb)
     every = pl.ds(0, SIDE)
-    sent = {}
+    sent, others = {}, {}
 
     def send(c, phase, pairs, to):
         copies = []
+        slot = sent.setdefault((c, phase), len(sent))
         for d in range(2):
             src, dst = pairs[d]
             copies.append(
                 pltpu.make_async_remote_copy(
                     src_ref=src,
                     dst_ref=dst,
-                    send_sem=ssem.at[c, phase, d],
-                    recv_sem=rsem.at[c, phase, d],
+                    send_sem=ssem.at[KINDS[phase]],
+                    recv_sem=rsem.at[slot],
                     device_id={"fsdp": to[d]},
                     device_id_type=MESH,
                 )
             )
         for copy in copies:
             copy.start()
-        sent[c, phase] = copies
+
+    def both(c, phase):
+        part = end if phase in SHORT else top
+        count = pl.ds(0, 2) if phase in FULL else 0
+        wide = phase in (5, 7, 9, 11)
+        wide = wide or (phase in (4, 6) and c not in SPLIT_GATHER)
+        wide = wide or (phase in (8, 10) and c not in SPLIT_SCATTER)
+        return wf.at[c, count, every, part] if wide else wf.at[c, 0, count, part]
 
     def arrive(c, phase):
-        for copy in sent[c, phase]:
-            copy.wait_recv()
+        brought = both(c, phase)
+        pltpu.make_async_copy(brought, brought, rsem.at[sent[c, phase]]).wait()
 
     def same(*refs):
         return [(r, r) for r in refs]
@@ -390,7 +400,7 @@
             nw[part, cols(c)] = jnp.where(chosen, mixed, stepped)
         copy = pltpu.make_async_copy(nw.at[:, cols(c)], nw_hbm.at[:, cols(c)], out_sem.at[c])
         copy.start()
-        sent["out", c] = copy
+        others["out", c] = copy
 
     spans = []
     base = 0
@@ -411,7 +421,7 @@
             device_id_type=MESH,
         )
         copy.start()
-        sent["outer", n] = copy
+        others["outer", n] = copy
 
     def halve(k):
         _, keep, give, size = spans[k]
@@ -424,7 +434,7 @@
 
     def halve_done(k):
         _, keep, give, size = spans[k]
-        sent["outer", k].wait_recv()
+        others["outer", k].wait_recv()
         kept = pl.ds(pl.multiple_of(keep, share), size)
         old_t[kept, :] = old_t[kept, :] + got[pl.ds(size, size), :]
 
@@ -483,8 +493,8 @@
         outer.append(lambda k=k: (halve_done(k - 1), halve(k)))
     outer.append(lambda: (halve_done(steps - 1), outer_update(), double(steps - 1)))
     for k in range(steps - 1, 0, -1):
-        outer.append(lambda k=k: (sent["outer", steps + k].wait_recv(), double(k - 1)))
-    outer.append(lambda: (sent["outer", steps].wait_recv(), outer_end()))
+        outer.append(lambda k=k: (others["outer", steps + k].wait_recv(), double(k - 1)))
+    outer.append(lambda: (others["outer", steps].wait_recv(), outer_end()))
 
     events = {
         "a0": a0,
@@ -521,14 +531,19 @@
     pl.semaphore_wait(barrier, 4 + len(bits))
     for event, c in ORDER:
         events[event](c)
-    for key, copies in sent.items():
-        if key[0] == "out":
-            copies.wait()
-        elif key[0] == "outer":
-            copies.wait_send()
+    for (key, _), copy in others.items():
+        if key == "out":
+            copy.wait()
         else:
-            for copy in copies:
-                copy.wait_send()
+            copy.wait_send()
+    chunks, three = pl.ds(0, nc), pl.ds(0, 3)
+    narrow, wide = wf.at[chunks, 0, three], wf.at[chunks, three]
+    for kind, (block, part) in enumerate(
+        [(narrow, top), (narrow, end), (wide, top), (wide, end)]
+        + [(wide, top), (wide, end), (narrow, top), (narrow, end)]
+    ):
+        gone = block.at[:, :, :, part] if block is wide else block.at[:, :, part]
+        pltpu.make_async_copy(gone, gone, ssem.at[kind]).wait()
 
 
 def shards(activations, teacher, weights, first_moment, second_moment, anchor, momentum, fragment):
@@ -541,6 +556,7 @@
     ra, rb = ROWS_A, rows - ROWS_A
     batch = tokens * lax.axis_size("fsdp")
     bits = replicas.bit_length() - 1
+    slots = CHUNKS * 16 + 6 * (len(SPLIT_GATHER) + len(SPLIT_SCATTER))
     vmem = pltpu.VMEM
     anywhere = pl.BlockSpec(memory_space=pl.ANY)
     inside = pl.BlockSpec(memory_space=pltpu.VMEM)
@@ -581,8 +597,8 @@
             vmem((whole, LANES), F32),
             pltpu.SemaphoreType.DMA((7,)),
             pltpu.SemaphoreType.DMA((CHUNKS,)),
-            pltpu.SemaphoreType.DMA((CHUNKS, PHASES, 2)),
-            pltpu.SemaphoreType.DMA((CHUNKS, PHASES, 2)),
+            pltpu.SemaphoreType.DMA((8,)),
+            pltpu.SemaphoreType.DMA((slots,)),
             pltpu.SemaphoreType.DMA((2 * bits,)),
             pltpu.SemaphoreType.DMA((2 * bits,)),
         ],

time: 154 us -> 151 us (0.981)
  Pallas kernels: 146 us -> 144 us
    pallas_call x1, Pallas kernels: 146 us -> 144 us  [shards(): pl.pallas_call(functools.partial(kernel, batch), out_shape=(jax.ShapeDtyp...]
where the time goes in v4:
time: 151 us; the launch traced here: 149 us
  Pallas kernels  144 us (95%)
  local copies, waits for them, and re-layouts  3.74 us (2%)
    pallas_call x1, Pallas kernels, shards(): pl.pallas_call(functools.partial(kernel, batch), out_shape=(jax.ShapeDtyp...  144 us
    unnamed x7, local copies, waits for them, and re-layouts  3.74 us

profile of v4, /device:TPU:32, one launch (start us, length us, event | category | flops | bytes accessed | tf_op | source)
XLA Modules:
  0.0 148.8 jit_solution(4670470334619601250)
XLA Ops:
  1.3 143.7 %shard_map.103 = (f32[288,1024]{1,0:T(8,128)}, f32[4,16,288]{2,1,0:T(8,128)}, f32[4,16,288]{2,1,0:T(8,128)}) custom-call(s32[1]{0:T(128)S(6)} %copy.14.frag_ref, bf16[640,4608]{1,0:T(8,128)(2,1)} %bitcast.10, bf16[640,1024]{1,0:T(8,128)(2,1)} %bitcast.11, f32[288,1024]{1,0:T(8,128)} %bitcast.13, f32[288,1024]{1,0:T(8,128)} %bitcast.14, ...), custom_call_target="tpu_custom_call" | custom-call | tf_op jit(solution)/shard_map/pallas_call | solution.py:563
  145.0 0.0 copy-start.1
  145.0 0.0 copy-start
  145.0 2.4 %copy.15 = f32[1,288,1024]{2,1,0:T(8,128)} copy(f32[1,288,1024]{2,1,0:T(8,128)} %bitcast.12) | data formatting | bytes 2359296
  147.5 0.0 copy-done.1
  147.5 0.6 copy.16
  148.1 0.0 copy-done
  148.1 0.6 copy.17
Async XLA Ops:
  145.0 2.5 %copy-start.1 = (f32[4,16,288]{2,1,0:T(8,128)S(1)}, f32[4,16,288]{2,1,0:T(8,128)}, u32[]{:S(2)}) copy-start(f32[4,16,288]{2,1,0:T(8,128)} %get-tuple-element.7) | copy-start | bytes 221188
  145.0 3.1 %copy-start = (f32[4,16,288]{2,1,0:T(8,128)S(1)}, f32[4,16,288]{2,1,0:T(8,128)}, u32[]{:S(2)}) copy-start(f32[4,16,288]{2,1,0:T(8,128)} %get-tuple-element.8) | copy-start | bytes 221188
